TPU v7x, 32 devices: a whole 2x2x4 slice. The times are simulated.
32 devices in a mesh: blk: 2 (over x), rows: 16 (over z, y, core).
Axes of the slice: x: 2, y: 2, z: 4, core: 2. Of those that a mesh axis runs over, the one named last changes fastest.
Arguments:
- queries: bfloat16 [32, 4, 8192], P('rows', None, 'blk'), may hold values from -36 to 36
- new_entries: bfloat16 [32, 4, 2, 1024], P('rows', None, None, 'blk'), may hold values from -9 to 9
- resident: bfloat16 [1792, 2, 16, 1024], P('rows', None, None, 'blk'), may hold values from -9 to 9
- swap_area: bfloat16 [256, 2, 16, 1024], P('rows', None, None, 'blk'), may hold values from -9 to 9
- swap_dest: int32 [256], P('rows'), may hold values from 0 to 15, as said below
- page_table: int32 [32, 64], P('rows'), may hold values from 0 to 143, as said below
- lengths: int32 [32], P('rows'), may hold values from 256 to 1024, as said below
- norm_gain: bfloat16 [8192], P('blk'), may hold values from 0.099609375 to 1.8984375
- gate_weight: bfloat16 [8192, 28672], P('blk', 'rows'), may hold values from -0.0625 to 0.0625
- up_weight: bfloat16 [8192, 28672], P('blk', 'rows'), may hold values from -0.0625 to 0.0625
- down_weight: bfloat16 [28672, 8192], P('rows', 'blk'), may hold values from -0.03125 to 0.03125
Outputs:
- attended: bfloat16 [32, 4, 8192], P('rows', None, 'blk')
- layer_out: bfloat16 [32, 4, 8192], P('rows', None, 'blk')
Inputs may be any that keep to these rules, and one draw needn't show every extreme that they name: `swap_dest`: every owner sends exactly 2 of its pages to each of 8 different owners (possibly itself), and every owner receives exactly 16 pages. `page_table`: the entries of the 2 rows of one owner name each of its 112 resident pages and each of the 16 pages that land there exactly once; an entry at or above 112 is 112 + s * 2 + k for the k-th page, in the order of the sender's pages, that owner s sends to the row's owner. `lengths`: some row has exactly 1024 cached positions.
All inputs are finite; a program needn't handle non-finite values.
Results may differ from a plain program's by a relative error of at most 0.0086.
Values may be sent and summed in bfloat16 or wider, within the bound.
A program may use at most 128 MiB of HBM per device.

v0:
```python
import math

import jax
import jax.numpy as jnp
from jax import lax
from jax.sharding import PartitionSpec as P

GQ = 8
HD = 128
PAGE = 16
CAP = 2


epsilon = 1e-05


def on_device(
    queries,
    new_entries,
    resident,
    swap_area,
    swap_dest,
    page_table,
    lengths,
    norm_gain,
    gate_weight,
    up_weight,
    down_weight,
):
    owners = lax.axis_size("rows")
    swap_count = swap_area.shape[0]
    page_width = swap_area.shape[1] * swap_area.shape[2] * swap_area.shape[3]
    flat_swap = swap_area.reshape(swap_count, page_width)
    target = swap_dest[:, None] == jnp.arange(owners, dtype=jnp.int32)[None, :]
    before = jnp.cumsum(target.astype(jnp.int32), axis=0) - 1
    page_rank = jnp.sum(jnp.where(target, before, 0), axis=1)
    send_slot = swap_dest * CAP + page_rank
    placement = (jnp.arange(owners * CAP, dtype=jnp.int32)[:, None] == send_slot[None, :]).astype(
        jnp.bfloat16
    )
    outgoing = jnp.dot(placement, flat_swap, preferred_element_type=jnp.float32).astype(
        jnp.bfloat16
    )
    outgoing = outgoing.reshape(owners, CAP, page_width)
    arrived = lax.all_to_all(outgoing, "rows", split_axis=0, concat_axis=0, tiled=True)
    page_store = jnp.concatenate(
        [resident.reshape(-1, page_width), arrived.reshape(owners * CAP, page_width)], axis=0
    )
    fetched = page_store[page_table]
    rows_here, pages_row = page_table.shape
    step_count = queries.shape[1]
    kv_heads = new_entries.shape[-1] // HD
    fetched = fetched.reshape(rows_here, pages_row, 2, PAGE, kv_heads, HD)
    cached_keys = fetched[:, :, 0].reshape(rows_here, pages_row * PAGE, kv_heads, HD)
    cached_values = fetched[:, :, 1].reshape(rows_here, pages_row * PAGE, kv_heads, HD)
    head_queries = queries.reshape(rows_here, step_count, kv_heads, GQ, HD)
    step_entries = new_entries.reshape(rows_here, step_count, 2, kv_heads, HD)
    score_scale = 1.0 / math.sqrt(HD)
    cached_scores = (
        jnp.einsum(
            "rskgd,rlkd->rkgsl", head_queries, cached_keys, preferred_element_type=jnp.float32
        )
        * score_scale
    )
    new_scores = (
        jnp.einsum(
            "rskgd,rtkd->rkgst",
            head_queries,
            step_entries[:, :, 0],
            preferred_element_type=jnp.float32,
        )
        * score_scale
    )
    visible = jnp.arange(pages_row * PAGE, dtype=jnp.int32)[None, :] < lengths[:, None]
    causal = jnp.arange(step_count)[None, :] <= jnp.arange(step_count)[:, None]
    cached_scores = jnp.where(visible[:, None, None, None, :], cached_scores, -1e30)
    new_scores = jnp.where(causal[None, None, None], new_scores, -1e30)
    row_peak = jnp.maximum(jnp.max(cached_scores, axis=-1), jnp.max(new_scores, axis=-1))[..., None]
    cached_exp = jnp.exp(cached_scores - row_peak)
    new_exp = jnp.exp(new_scores - row_peak)
    row_total = (jnp.sum(cached_exp, axis=-1) + jnp.sum(new_exp, axis=-1))[..., None]
    cached_weights = (cached_exp / row_total).astype(jnp.bfloat16)
    new_weights = (new_exp / row_total).astype(jnp.bfloat16)
    mixed_heads = jnp.einsum(
        "rkgsl,rlkd->rskgd", cached_weights, cached_values, preferred_element_type=jnp.float32
    )
    mixed_heads = mixed_heads + jnp.einsum(
        "rkgst,rtkd->rskgd", new_weights, step_entries[:, :, 1], preferred_element_type=jnp.float32
    )
    attended = mixed_heads.reshape(rows_here, step_count, -1).astype(jnp.bfloat16)
    local_tokens = attended.reshape(rows_here * step_count, -1)
    gathered = lax.all_gather(local_tokens, "rows", axis=0, tiled=True)
    gathered_wide = gathered.astype(jnp.float32)
    squares = jnp.sum(gathered_wide * gathered_wide, axis=1)
    normed = (gathered_wide * norm_gain.astype(jnp.float32)[None, :]).astype(jnp.bfloat16)
    gate_part = jnp.dot(normed, gate_weight, preferred_element_type=jnp.float32)
    up_part = jnp.dot(normed, up_weight, preferred_element_type=jnp.float32)
    width_total = gathered.shape[1] * lax.axis_size("blk")
    gate_sum, up_sum, square_sum = lax.psum((gate_part, up_part, squares), "blk")
    factor = lax.rsqrt(square_sum / width_total + epsilon)[:, None]
    hidden = (jax.nn.silu(factor * gate_sum) * (factor * up_sum)).astype(jnp.bfloat16)
    down_sum = lax.psum_scatter(
        jnp.dot(hidden, down_weight, preferred_element_type=jnp.float32),
        "rows",
        scatter_dimension=0,
        tiled=True,
    )
    layer_out = (local_tokens.astype(jnp.float32) + down_sum).astype(jnp.bfloat16)
    return (attended, layer_out.reshape(rows_here, step_count, -1))


def solution(mesh):
    placed = (
        P("rows", None, "blk"),
        P("rows", None, None, "blk"),
        P("rows", None, None, "blk"),
        P("rows", None, None, "blk"),
        P("rows"),
        P("rows", None),
        P("rows"),
        P("blk"),
        P("blk", "rows"),
        P("blk", "rows"),
        P("rows", "blk"),
    )
    return jax.shard_map(
        on_device,
        mesh=mesh,
        in_specs=placed,
        out_specs=(P("rows", None, "blk"), P("rows", None, "blk")),
        check_vma=False,
    )
```

profile of v0, /device:TPU:0, one launch (start us, length us, event | category | flops | bytes accessed | tf_op | source)
XLA Modules:
  0.0 267.2 jit_solution(15961150428196964114)
XLA Ops:
  7.2 1.3 copy.34
  8.5 0.7 fusion.24
  9.3 0.8 select_reduce_fusion
  10.1 0.7 multiply_add_fusion
  11.2 1.5 reshape.78
  12.7 7.4 %all-to-all-start = ((bf16[16,2,16384]{2,1,0:T(2,128)(2,1)}), bf16[16,2,16384]{2,1,0:T(2,128)(2,1)S(1)}, u32[]{:S(2)}, u32[]{:S(2)}) async-start(bf16[16,2,16384]{2,1,0:T(2,128)(2,1)} %reshape.78), calls=%async_computation | async-start | bytes 2097152 | tf_op jit(solution)/shard_map/all_to_all | solution.py:45
  20.2 6.3 %copy.33 = bf16[14,8,32,512]{3,1,2,0:T(8,128)(2,1)} copy(bf16[14,8,32,512]{3,2,1,0:T(8,128)(2,1)} %bitcast.56) | data formatting | bytes 7340032
  27.3 15.7 %all-to-all-done = bf16[16,2,16384]{2,1,0:T(2,128)(2,1)S(1)} async-done(((bf16[16,2,16384]{2,1,0:T(2,128)(2,1)}), bf16[16,2,16384]{2,1,0:T(2,128)(2,1)S(1)}, u32[]{:S(2)}, u32[]{:S(2)}) %all-to-all-start) | async-done | bytes 1048608 | tf_op jit(solution)/shard_map/all_to_all | solution.py:45
  43.4 4.5 %pad_maximum_fusion = bf16[144,16384]{1,0:T(8,128)(2,1)} fusion(bf16[32,16384]{1,0:T(8,128)(2,1)S(1)} %reshape.79, bf16[112,16384]{1,0:T(8,128)(2,1)} %bitcast.54), kind=kLoop, calls=%fused_computation.2 | loop fusion | flops 9437184 | bytes 9437184 | tf_op jit(solution)/shard_map/concatenate | solution.py:46
  48.0 11.8 %gather_fusion = bf16[128,16384]{1,0:T(8,128)(2,1)} fusion(bf16[144,16384]{1,0:T(8,128)(2,1)} %pad_maximum_fusion, s32[1024]{0:T(1024)S(1)} %pad_clamp_fusion), kind=kCustom, calls=%fused_computation | custom fusion | bytes 8389120 | tf_op jit(solution)/shard_map/gather | solution.py:49
  59.7 7.7 %reshape.80 = bf16[2,64,2,16,4,128]{5,4,3,2,1,0:T(4,128)(2,1)} reshape(bf16[128,16384]{1,0:T(8,128)(2,1)} %gather_fusion) | data formatting | bytes 8388608 | tf_op jit(solution)/shard_map/reshape | solution.py:53
  67.5 3.6 %fusion.26 = (bf16[2,64,1,16,4,128]{5,4,3,2,1,0:T(4,128)(2,1)S(1)}, bf16[2,64,1,16,4,128]{5,4,3,2,1,0:T(4,128)(2,1)S(1)}) fusion(bf16[2,64,2,16,4,128]{5,4,3,2,1,0:T(4,128)(2,1)} %reshape.80), kind=kLoop, calls=%fused_computation.50 | loop fusion | bytes 8388608 | tf_op jit(solution)/shard_map/slice | solution.py:55
  71.3 0.9 fusion.28
  73.7 0.7 convert_element_type.47
  74.7 40.0 %all-gather.2.cloned.1.call-done = bf16[128,4096]{1,0:T(8,128)(2,1)} async-done(((bf16[8,4096]{1,0:T(8,128)(2,1)}), bf16[128,4096]{1,0:T(8,128)(2,1)}) %all-gather.2.cloned.1.call-update) | async-done | bytes 1048592 | tf_op jit(solution)/shard_map/all_gather | solution.py:92
  114.6 8.6 %fusion.11 = f32[128,1792]{1,0:T(8,128)} fusion(bf16[4096,1792]{1,0:T(8,128)(2,1)} %param.19, bf16[128,4096]{1,0:T(8,128)(2,1)} %all-gather.2.cloned.1.call-done, f32[4096]{0:T(1024)S(1)} %convert_element_type.50), kind=kOutput, calls=%fused_computation.22 | convolution fusion | flops 1880621056 | bytes 16662528 | tf_op jit(solution)/shard_map/dot_general | solution.py:96
  123.3 8.2 %fusion.9 = f32[128,1792]{1,0:T(8,128)} fusion(bf16[4096,1792]{1,0:T(8,128)(2,1)} %param.20, bf16[128,4096]{1,0:T(8,128)(2,1)S(1)} %copy-done, f32[4096]{0:T(1024)S(1)} %convert_element_type.50), kind=kOutput, calls=%fused_computation.21 | convolution fusion | flops 1880621056 | bytes 16662528 | tf_op jit(solution)/shard_map/dot_general | solution.py:97
  131.8 4.9 %psum.21 = f32[128]{0:T(128)S(1)} all-reduce(f32[128]{0:T(128)S(1)} %fusion), channel_id=1, replica_groups=mesh['blk'=2,'rows'=16] {'blk'}, use_global_device_ids=true, to_apply=%region_7.8 | all-reduce | flops 128 | bytes 1024 | tf_op jit(solution)/shard_map/psum | solution.py:99
  136.7 51.2 %all-reduce.3.cloned.1.call-done = (f32[128,1792]{1,0:T(8,128)}, f32[128,1792]{1,0:T(8,128)}) async-done(((f32[128,1792]{1,0:T(8,128)}, f32[128,1792]{1,0:T(8,128)}), (f32[128,1792]{1,0:T(8,128)}, f32[128,1792]{1,0:T(8,128)})) %all-reduce.3.cloned.1.call-update) | async-done | bytes 1835024 | tf_op jit(solution)/shard_map/psum | solution.py:99
  187.9 9.3 %fusion.15 = f32[128,4096]{1,0:T(8,128)} fusion(bf16[1792,4096]{1,0:T(8,128)(2,1)} %param.21, f32[128,1792]{1,0:T(8,128)} %get-tuple-element.2, f32[128,1792]{1,0:T(8,128)} %get-tuple-element.3, f32[128]{0:T(128)S(1)} %add_rsqrt_fusion), kind=kOutput, calls=%fused_computation.25 | convolution fusion | flops 1880883200 | bytes 18612736 | tf_op jit(solution)/shard_map/dot_general | solution.py:103
  197.3 0.7 convert_element_type.46
  198.0 61.1 %reduce-scatter.2.cloned.1.call-done = f32[8,4096]{1,0:T(8,128)} async-done(((f32[128,4096]{1,0:T(8,128)}), f32[8,4096]{1,0:T(8,128)}) %reduce-scatter.2.cloned.1.call-update) | async-done | bytes 131088 | tf_op jit(solution)/shard_map/reduce_scatter | solution.py:102
  259.1 0.9 add_convert_fusion
  260.0 0.7 reshape.83
  (44 shorter events, 4.0 us)
Async XLA Ops:
  12.7 30.3 %all-to-all-start = ((bf16[16,2,16384]{2,1,0:T(2,128)(2,1)}), bf16[16,2,16384]{2,1,0:T(2,128)(2,1)S(1)}, u32[]{:S(2)}, u32[]{:S(2)}) async-start(bf16[16,2,16384]{2,1,0:T(2,128)(2,1)} %reshape.78), calls=%async_computation | async-start | bytes 2097152 | tf_op jit(solution)/shard_map/all_to_all | solution.py:45
  20.1 6.4 %copy-start.5 = (s32[2,64]{1,0:T(2,128)S(1)}, s32[2,64]{1,0:T(2,128)}, u32[]{:S(2)}) copy-start(s32[2,64]{1,0:T(2,128)} %param.16) | copy-start | bytes 1540
  20.1 6.5 %copy-start.2 = (bf16[2,4,4096]{2,1,0:T(4,128)(2,1)S(1)}, bf16[2,4,4096]{2,1,0:T(4,128)(2,1)}, u32[]{:S(2)}) copy-start(bf16[2,4,4096]{2,1,0:T(4,128)(2,1)} %param.11) | copy-start | bytes 196612
  20.1 6.6 %copy-start.3 = (bf16[2,4,2,512]{3,2,1,0:T(2,128)(2,1)S(1)}, bf16[2,4,2,512]{3,2,1,0:T(2,128)(2,1)}, u32[]{:S(2)}) copy-start(bf16[2,4,2,512]{3,2,1,0:T(2,128)(2,1)} %param.12) | copy-start | bytes 49156
  20.1 6.6 %copy-start.6 = (s32[2]{0:T(128)S(1)}, s32[2]{0:T(128)}, u32[]{:S(2)}) copy-start(s32[2]{0:T(128)} %param.17) | copy-start | bytes 28
  20.1 94.5 %all-gather.2.cloned.1.call-start = ((), (), s32[]{:S(2)}) async-start(), calls=%async_computation.2 | async-start | bytes 1114112 | tf_op jit(solution)/shard_map/all_gather | solution.py:92
  72.9 1.7 copy-start.4
  74.4 113.6 %all-reduce.3.cloned.1.call-start = ((), (), s32[]{:S(2)}) async-start(), calls=%async_computation.4 | async-start | bytes 3670016 | tf_op jit(solution)/shard_map/psum | solution.py:99
  114.6 8.6 %copy-start = (bf16[128,4096]{1,0:T(8,128)(2,1)S(1)}, bf16[128,4096]{1,0:T(8,128)(2,1)}, u32[]{:S(2)}) copy-start(bf16[128,4096]{1,0:T(8,128)(2,1)} %all-gather.2.cloned.1.call-done) | copy-start | bytes 3145732
  131.5 127.6 %reduce-scatter.2.cloned.1.call-start = ((), (), s32[]{:S(2)}) async-start(), calls=%async_computation.3 | async-start | bytes 2228224 | tf_op jit(solution)/shard_map/reduce_scatter | solution.py:102
  187.9 71.1 %copy-start.1 = (bf16[8,4096]{1,0:T(8,128)(2,1)S(1)}, bf16[8,4096]{1,0:T(8,128)(2,1)}, u32[]{:S(2)}) copy-start(bf16[8,4096]{1,0:T(8,128)(2,1)} %convert_element_type.47) | copy-start | bytes 196612
Sparse Core Ops, SparseCore 0:
  74.5 40.1 all-gather.1
  131.6 56.3 all-reduce.2
  197.4 61.5 reduce-scatter.1
where the time goes:
time: 268 us; the launch traced here: 267 us
  waiting for transfers between devices  168 us (63%)
  local copies, waits for them, and re-layouts  35.5 us (13%)
  matrix products  28.6 us (11%)
  between operations  13.9 us (5%)
  other arithmetic  8.48 us (3%)
  starting transfers between devices  7.73 us (3%)
  blocking collectives  4.94 us (2%)
    reduce_scatter x1, waiting for transfers between devices, on_device(): lax.psum_scatter(jnp.dot(hidden, down_weight, preferred_element_type=jnp....  61.1 us
    psum x1, waiting for transfers between devices, on_device(): lax.psum((gate_part, up_part, squares), 'blk')  51.2 us
    all_gather x1, waiting for transfers between devices, on_device(): gathered = lax.all_gather(local_tokens, 'rows', axis=0, tiled=True)  40 us
    all_to_all x1, waiting for transfers between devices, on_device(): lax.all_to_all(outgoing, 'rows', split_axis=0, concat_axis=0, tiled=True)  15.7 us
    gather x1, local copies, waits for them, and re-layouts, on_device(): fetched = page_store[page_table]  11.8 us
    dot_general x1, matrix products, on_device(): jnp.dot(hidden, down_weight, preferred_element_type=jnp.float32)  9.34 us
    dot_general x1, matrix products, on_device(): gate_part = jnp.dot(normed, gate_weight, preferred_element_type=jnp.float32)  8.62 us
    unnamed x18, local copies, waits for them, and re-layouts  8.26 us
  transfers between devices with their start and end apart: 4, of which 4 were waited for; matrix products, arithmetic and copies ran while one was open for 3% of the time, Pallas kernels for 0%

commit v1 on v0

v1 whole, which is shorter than its diff:
```python
import functools
import math

import jax
import jax.numpy as jnp
from jax import lax
from jax.experimental import pallas as pl
from jax.experimental.pallas import tpu as pltpu
from jax.sharding import PartitionSpec as P

GQ = 8
HD = 128
PAGE = 16
CAP = 2
TOK = 8
epsilon = 1e-05
MESH = pl.DeviceIdType.MESH
NEG = -1e30


def pack_kernel(dest_ref, swap_ref, out_ref, count_ref, source_ref, sems):
    pages = swap_ref.shape[0]
    slots = out_ref.shape[0]

    @pl.loop(0, slots)
    def _(i):
        source_ref[i] = 0

    @pl.loop(0, slots // CAP)
    def _(i):
        count_ref[i] = 0

    @pl.loop(0, pages)
    def _(i):
        owner = dest_ref[i]
        rank = count_ref[owner]
        count_ref[owner] = rank + 1
        source_ref[owner * CAP + rank] = i

    def copy(i):
        return pltpu.make_async_copy(swap_ref.at[source_ref[i]], out_ref.at[i], sems.at[i])

    @pl.loop(0, slots)
    def _(i):
        copy(i).start()

    @pl.loop(0, slots)
    def _(i):
        copy(i).wait()


def pack_pages(swap_dest, swap_area, owners):
    return pl.pallas_call(
        pack_kernel,
        out_shape=jax.ShapeDtypeStruct((owners * CAP,) + swap_area.shape[1:], swap_area.dtype),
        in_specs=[pl.BlockSpec(memory_space=pltpu.SMEM), pl.BlockSpec(memory_space=pl.ANY)],
        out_specs=pl.BlockSpec(memory_space=pl.ANY),
        scratch_shapes=[
            pltpu.SMEM((owners,), jnp.int32),
            pltpu.SMEM((owners * CAP,), jnp.int32),
            pltpu.SemaphoreType.DMA((owners * CAP,)),
        ],
    )(swap_dest, swap_area)


def layer_kernel(
    cfg,
    q_ref, new_ref, res_bias_ref, swap_bias_ref, gain_ref,
    resident_ref, outgoing_ref, wg_hbm, wu_hbm, wd_hbm,
    att_out, layer_out,
    kv, arrived, wg, wu, wd, att, ag, lhs, gu32, gu16, gu_in, sq_out, sq_in, hid,
    acc, rs, rs_core, rs_y, rs_z,
    kv_sem, w_sem, own_sem,
    sw_s, sw_r, az_s, az_r, ay_s, ay_r, ac_s, ac_r,
    gu_s, gu_r, sq_s, sq_r, hd_s, hd_r,
    rc_s, rc_r, ry_s, ry_r, rz_s, rz_r,
):
    nr, nb, steps, width, parts, fc = cfg
    w2 = width // 2
    zs = nr // 4
    nt, _, tn = ag.shape
    nc = gu32.shape[0]
    kh = width // (GQ * HD)
    rows_here = TOK // steps
    tokens = nr * TOK
    part = tokens // nb
    me = lax.axis_index("rows")
    b = lax.axis_index("blk")
    z, y, c = me // 4, (me // 2) % 2, me % 2

    def row_of(z_, y_, c_):
        return {"rows": z_ * 4 + y_ * 2 + c_}

    kv_copy = pltpu.make_async_copy(resident_ref, kv, kv_sem)
    kv_copy.start()

    def weight_copies(i):
        src, dst = ((wg_hbm, wg), (wu_hbm, wu), (wd_hbm, wd))[i]
        step = dst.shape[0] // parts
        return [
            pltpu.make_async_copy(
                src.at[pl.ds(j * step, step)], dst.at[pl.ds(j * step, step)], w_sem.at[i * parts + j]
            )
            for j in range(parts)
        ]

    barrier = pltpu.get_barrier_semaphore()

    @pl.loop(1, nr)
    def _(k):
        pl.semaphore_signal(
            barrier, inc=1, device_id={"rows": lax.rem(me + k, nr)}, device_id_type=MESH
        )

    for k in range(1, nb):
        pl.semaphore_signal(
            barrier, inc=1, device_id={"blk": lax.rem(b + k, nb)}, device_id_type=MESH
        )
    pl.semaphore_wait(barrier, nr + nb - 2)

    def remote(src, dst, send, recv, device):
        return pltpu.make_async_remote_copy(
            src_ref=src, dst_ref=dst, send_sem=send, recv_sem=recv,
            device_id=device, device_id_type=MESH,
        )

    def swap_copy(k):
        dest = lax.rem(me + k, nr)
        return remote(
            outgoing_ref.at[dest], arrived.at[me], sw_s.at[k], sw_r.at[k], {"rows": dest}
        )

    own_copy = pltpu.make_async_copy(outgoing_ref.at[me], arrived.at[me], own_sem)
    own_copy.start()

    @pl.loop(1, nr)
    def _(k):
        swap_copy(k).start()

    for i in range(3):
        for copy in weight_copies(i):
            copy.start()

    scale = 1.0 / math.sqrt(HD)
    token_row = lax.broadcasted_iota(jnp.int32, (TOK, 1), 0) // steps

    def token_mask(ref):
        mask = jnp.broadcast_to(ref[0:1, :], (TOK, ref.shape[1]))
        for r in range(1, rows_here):
            mask = jnp.where(token_row == r, ref[r : r + 1, :], mask)
        return mask[None] > 0.5

    def scores(qk, keys, mask):
        s = lax.dot_general(
            qk, keys, (((1,), (1,)), ((), ())), preferred_element_type=jnp.float32
        )
        s = (s * scale).reshape(GQ, TOK, s.shape[1])
        return jnp.where(mask, s, NEG)

    def weigh(p, values):
        p2 = p.reshape(GQ * TOK, p.shape[2]).astype(jnp.bfloat16)
        o = jnp.dot(p2, values, preferred_element_type=jnp.float32)
        return o.reshape(GQ, TOK, HD)

    tok_i = lax.broadcasted_iota(jnp.int32, (TOK, new_ref.shape[1]), 0)
    key_i = lax.broadcasted_iota(jnp.int32, (TOK, new_ref.shape[1]), 1)
    new_mask = (
        (tok_i // steps == key_i // steps) & (key_i % steps <= tok_i % steps) & (key_i < TOK)
    )[None]

    q32 = q_ref[...].astype(jnp.float32)
    heads = []
    for k in range(kh):
        heads.append(
            jnp.concatenate(
                [q32[:, (k * GQ + g) * HD : (k * GQ + g + 1) * HD] for g in range(GQ)], axis=0
            ).astype(jnp.bfloat16)
        )
    kv_copy.wait()
    res_mask = token_mask(res_bias_ref)
    n_res = kv.shape[0] * PAGE
    state = []
    for k in range(kh):
        lanes = slice(k * HD, (k + 1) * HD)
        s1 = scores(heads[k], kv[:, 0, :, lanes].reshape(n_res, HD), res_mask)
        s2 = scores(heads[k], new_ref[0, :, lanes], new_mask)
        m = jnp.maximum(jnp.max(s1, axis=-1, keepdims=True), jnp.max(s2, axis=-1, keepdims=True))
        p1, p2 = jnp.exp(s1 - m), jnp.exp(s2 - m)
        l = jnp.sum(p1, axis=-1, keepdims=True) + jnp.sum(p2, axis=-1, keepdims=True)
        o = weigh(p1, kv[:, 1, :, lanes].reshape(n_res, HD)) + weigh(p2, new_ref[1, :, lanes])
        state.append((m, l, o))

    own_copy.wait()

    @pl.loop(1, nr)
    def _(k):
        swap_copy(k).wait_recv()

    swap_mask = token_mask(swap_bias_ref)
    n_swap = nr * CAP * PAGE
    for k in range(kh):
        lanes = slice(k * HD, (k + 1) * HD)
        m1, l1, o1 = state[k]
        s = scores(heads[k], arrived[:, :, 0, :, lanes].reshape(n_swap, HD), swap_mask)
        m = jnp.maximum(m1, jnp.max(s, axis=-1, keepdims=True))
        p = jnp.exp(s - m)
        old = jnp.exp(m1 - m)
        l = l1 * old + jnp.sum(p, axis=-1, keepdims=True)
        o = o1 * old + weigh(p, arrived[:, :, 1, :, lanes].reshape(n_swap, HD))
        o = o / l
        for g in range(GQ):
            att[:, (k * GQ + g) * HD : (k * GQ + g + 1) * HD] = o[g]

    def slots(first, count):
        return pl.ds(pl.multiple_of(first * 16, 16), count * 16)

    column = (c * 2 + y) * zs

    def ag_z(n, k):
        zp = lax.rem(z + k, zs)
        piece = ag.at[n, slots(column + z, 1)]
        return remote(piece, piece, az_s.at[n, k], az_r.at[n, k], row_of(zp, y, c))

    def ag_y(n):
        piece = ag.at[n, slots(column, zs)]
        return remote(piece, piece, ay_s.at[n], ay_r.at[n], row_of(z, 1 - y, c))

    def ag_c(n):
        piece = ag.at[n, slots(c * 2 * zs, 2 * zs)]
        return remote(piece, piece, ac_s.at[n], ac_r.at[n], row_of(z, y, 1 - c))

    for n in range(nt):
        left, right = slice(n * tn, (n + 1) * tn), slice(w2 + n * tn, w2 + (n + 1) * tn)
        ag[n, slots(column + z, 1), :] = jnp.concatenate(
            [att[:, left], att[:, right]], axis=0
        ).astype(jnp.bfloat16)
        for k in range(1, zs):
            ag_z(n, k).start()
    att_out[...] = att[...].astype(jnp.bfloat16)
    for n in range(nt):
        for k in range(1, zs):
            ag_z(n, k).wait_recv()
        ag_y(n).start()
    for n in range(nt):
        ag_y(n).wait_recv()
        ag_c(n).start()
    squares = jnp.zeros((tokens, 1), jnp.float32)
    for n in range(nt):
        ag_c(n).wait_recv()
        wide = ag[n].astype(jnp.float32).reshape(nr, 2, TOK, tn)
        for side in range(2):
            x = wide[:, side].reshape(tokens, tn)
            squares = squares + jnp.sum(x * x, axis=1, keepdims=True)
            lanes = slice(side * w2 + n * tn, side * w2 + (n + 1) * tn)
            lhs[:, lanes] = (x * gain_ref[:, lanes].astype(jnp.float32)).astype(jnp.bfloat16)
    sq_out[...] = jnp.broadcast_to(squares, sq_out.shape)

    def share(p):
        return pl.ds(pl.multiple_of(p * part, 16), part)

    def sq_copy(k):
        p = lax.rem(b + k, nb)
        return remote(
            sq_out.at[share(p)], sq_in.at[k - 1], sq_s.at[k - 1], sq_r.at[k - 1], {"blk": p}
        )

    def gu_copy(j, k):
        p = lax.rem(b + k, nb)
        return remote(
            gu16.at[j, :, share(p)], gu_in.at[j, k - 1],
            gu_s.at[j, k - 1], gu_r.at[j, k - 1], {"blk": p},
        )

    def hid_copy(j, k):
        p = lax.rem(b + k, nb)
        piece = hid.at[j, share(b)]
        return remote(piece, piece, hd_s.at[j, k - 1], hd_r.at[j, k - 1], {"blk": p})

    for k in range(1, nb):
        sq_copy(k).start()
    for copy in weight_copies(0) + weight_copies(1):
        copy.wait()

    def project(j, carry):
        cols = pl.ds(pl.multiple_of(j * fc, fc), fc) if nc > 1 else slice(None)
        for i, w in enumerate((wg, wu)):
            value = jnp.dot(lhs[...], w[:, cols], preferred_element_type=jnp.float32)
            gu32[j, i] = value
            gu16[j, i] = value.astype(jnp.bfloat16)
        for k in range(1, nb):
            gu_copy(j, k).start()
        return carry

    lax.fori_loop(0, nc, project, 0)

    total = sq_out[share(b), 0:1]
    for k in range(1, nb):
        sq_copy(k).wait_recv()
        total = total + sq_in[k - 1, :, 0:1]
    factor = lax.rsqrt(total / (width * nb) + epsilon)

    def activate(j, carry):
        gate = gu32[j, 0, share(b), :]
        up = gu32[j, 1, share(b), :]
        for k in range(1, nb):
            gu_copy(j, k).wait_recv()
            gate = gate + gu_in[j, k - 1, 0].astype(jnp.float32)
            up = up + gu_in[j, k - 1, 1].astype(jnp.float32)
        gate = gate * factor
        up = up * factor
        hid[j, share(b), :] = (gate / (1.0 + jnp.exp(-gate)) * up).astype(jnp.bfloat16)
        for k in range(1, nb):
            hid_copy(j, k).start()
        return carry

    lax.fori_loop(0, nc, activate, 0)
    for copy in weight_copies(2):
        copy.wait()

    @pl.loop(0, nc)
    def _(j):
        for k in range(1, nb):
            hid_copy(j, k).wait_recv()

    def rs_c_copy(n):
        return remote(
            rs.at[n, slots((1 - c) * 2 * zs, 2 * zs)], rs_core.at[n],
            rc_s.at[n], rc_r.at[n], row_of(z, y, 1 - c),
        )

    def rs_y_copy(n):
        return remote(
            rs.at[n, slots((c * 2 + 1 - y) * zs, zs)], rs_y.at[n],
            ry_s.at[n], ry_r.at[n], row_of(z, 1 - y, c),
        )

    def rs_z_copy(n, k):
        zp = lax.rem(z + k, zs)
        return remote(
            rs.at[n, slots(column + zp, 1)], rs_z.at[n, k - 1],
            rz_s.at[n, k - 1], rz_r.at[n, k - 1], row_of(zp, y, c),
        )

    def down(n, carry):
        sides = []
        for side in range(2):
            cols = pl.ds(pl.multiple_of(side * w2 + n * tn, tn), tn)
            value = jnp.zeros((tokens, tn), jnp.float32)
            for j in range(nc):
                value = value + jnp.dot(
                    hid[j], wd[j * fc : (j + 1) * fc, cols], preferred_element_type=jnp.float32
                )
            sides.append(value.reshape(nr, TOK, tn))
        value = jnp.concatenate(sides, axis=1).reshape(nr * 16, tn)
        acc[n] = value
        rs[n] = value.astype(jnp.bfloat16)
        rs_c_copy(n).start()
        return carry

    lax.fori_loop(0, nt, down, 0)

    for n in range(nt):
        rs_c_copy(n).wait_recv()
        mine = slots(c * 2 * zs, 2 * zs)
        value = acc[n, mine, :] + rs_core[n].astype(jnp.float32)
        acc[n, mine, :] = value
        rs[n, mine, :] = value.astype(jnp.bfloat16)
        rs_y_copy(n).start()
    for n in range(nt):
        rs_y_copy(n).wait_recv()
        mine = slots(column, zs)
        value = acc[n, mine, :] + rs_y[n].astype(jnp.float32)
        acc[n, mine, :] = value
        rs[n, mine, :] = value.astype(jnp.bfloat16)
        for k in range(1, zs):
            rs_z_copy(n, k).start()
    for n in range(nt):
        value = acc[n, slots(column + z, 1), :]
        for k in range(1, zs):
            rs_z_copy(n, k).wait_recv()
            value = value + rs_z[n, k - 1].astype(jnp.float32)
        for side in range(2):
            lanes = slice(side * w2 + n * tn, side * w2 + (n + 1) * tn)
            base = att[:, lanes].astype(jnp.bfloat16).astype(jnp.float32)
            att[:, lanes] = base + value[side * TOK : (side + 1) * TOK]
    layer_out[...] = att[...].astype(jnp.bfloat16)

    @pl.loop(1, nr)
    def _(k):
        swap_copy(k).wait_send()

    for k in range(1, nb):
        sq_copy(k).wait_send()

    @pl.loop(0, nc)
    def _(j):
        for k in range(1, nb):
            gu_copy(j, k).wait_send()
            hid_copy(j, k).wait_send()

    for n in range(nt):
        for k in range(1, zs):
            ag_z(n, k).wait_send()
            rs_z_copy(n, k).wait_send()
        ag_y(n).wait_send()
        ag_c(n).wait_send()
        rs_c_copy(n).wait_send()
        rs_y_copy(n).wait_send()


def on_device(
    queries,
    new_entries,
    resident,
    swap_area,
    swap_dest,
    page_table,
    lengths,
    norm_gain,
    gate_weight,
    up_weight,
    down_weight,
):
    nr, nb = lax.axis_size("rows"), lax.axis_size("blk")
    rows_here, steps, width = queries.shape
    kvw = new_entries.shape[-1]
    hidden = gate_weight.shape[1]
    res_pages = resident.shape[0]
    pages_row = page_table.shape[1]
    zs = nr // 4
    w2 = width // 2
    tn = min(512, w2)
    nt = w2 // tn
    fc = 256 if hidden % 256 == 0 else hidden
    nc = hidden // fc
    tokens = nr * TOK
    part = tokens // nb
    parts = 4

    outgoing = pack_pages(swap_dest, swap_area, nr).reshape(nr, CAP, 2, PAGE, kvw)

    total_pages = res_pages + nr * CAP
    place = jnp.arange(total_pages * PAGE, dtype=jnp.int32)
    position = jnp.arange(pages_row, dtype=jnp.int32)[:, None] * PAGE + (place % PAGE)[None, :]
    seen = jnp.any(
        (page_table[:, :, None] == (place // PAGE)[None, None, :])
        & (position[None] < lengths[:, None, None]),
        axis=1,
    ).astype(jnp.float32)
    res_bias = seen[:, : res_pages * PAGE]
    swap_bias = seen[:, res_pages * PAGE :]
    new_kv = jnp.pad(
        new_entries.transpose(2, 0, 1, 3).reshape(2, TOK, kvw), ((0, 0), (0, 128 - TOK), (0, 0))
    )

    bf, f32 = jnp.bfloat16, jnp.float32
    dma = pltpu.SemaphoreType.DMA
    vm = pl.BlockSpec(memory_space=pltpu.VMEM)
    hbm = pl.BlockSpec(memory_space=pl.ANY)
    peers = max(nb - 1, 1)
    zp = max(zs - 1, 1)
    pair = lambda *shape: [dma(shape), dma(shape)]
    attended, layer = pl.pallas_call(
        functools.partial(layer_kernel, (nr, nb, steps, width, parts, fc)),
        out_shape=[jax.ShapeDtypeStruct((TOK, width), bf)] * 2,
        in_specs=[vm] * 5 + [hbm] * 5,
        out_specs=[vm] * 2,
        scratch_shapes=[
            pltpu.VMEM(resident.shape, bf),
            pltpu.VMEM((nr, CAP, 2, PAGE, kvw), bf),
            pltpu.VMEM(gate_weight.shape, bf),
            pltpu.VMEM(up_weight.shape, bf),
            pltpu.VMEM(down_weight.shape, bf),
            pltpu.VMEM((TOK, width), f32),
            pltpu.VMEM((nt, nr * 16, tn), bf),
            pltpu.VMEM((tokens, width), bf),
            pltpu.VMEM((nc, 2, tokens, fc), f32),
            pltpu.VMEM((nc, 2, tokens, fc), bf),
            pltpu.VMEM((nc, peers, 2, part, fc), bf),
            pltpu.VMEM((tokens, 128), f32),
            pltpu.VMEM((peers, part, 128), f32),
            pltpu.VMEM((nc, tokens, fc), bf),
            pltpu.VMEM((nt, nr * 16, tn), f32),
            pltpu.VMEM((nt, nr * 16, tn), bf),
            pltpu.VMEM((nt, 2 * zs * 16, tn), bf),
            pltpu.VMEM((nt, zs * 16, tn), bf),
            pltpu.VMEM((nt, zp, 16, tn), bf),
            dma,
            dma((3 * parts,)),
            dma,
        ]
        + pair(nr) + pair(nt, zs) + pair(nt) + pair(nt)
        + pair(nc, peers) + pair(peers) + pair(nc, peers)
        + pair(nt) + pair(nt) + pair(nt, zp),
        compiler_params=pltpu.CompilerParams(
            collective_id=0, has_side_effects=True, vmem_limit_bytes=62 * 1024 * 1024
        ),
        cost_estimate=pl.CostEstimate(
            flops=6 * tokens * width * hidden,
            bytes_accessed=6 * width * hidden,
            transcendentals=tokens * hidden,
        ),
    )(
        queries.reshape(TOK, width), new_kv, res_bias, swap_bias, norm_gain.reshape(1, width),
        resident, outgoing, gate_weight, up_weight, down_weight,
    )
    shape = (rows_here, steps, width)
    return attended.reshape(shape), layer.reshape(shape)


def solution(mesh):
    placed = (
        P("rows", None, "blk"),
        P("rows", None, None, "blk"),
        P("rows", None, None, "blk"),
        P("rows", None, None, "blk"),
        P("rows"),
        P("rows", None),
        P("rows"),
        P("blk"),
        P("blk", "rows"),
        P("blk", "rows"),
        P("rows", "blk"),
    )
    return jax.shard_map(
        on_device,
        mesh=mesh,
        in_specs=placed,
        out_specs=(P("rows", None, "blk"), P("rows", None, "blk")),
        check_vma=False,
    )
```

time: 268 us -> 124 us (0.46)
  waiting for transfers between devices: 168 us -> 0 us
  Pallas kernels: 0 us -> 113 us
  matrix products: 28.6 us -> 0 us
  local copies, waits for them, and re-layouts: 35.5 us -> 8.45 us
  between operations: 13.9 us -> 0.69 us
  starting transfers between devices: 7.73 us -> 0 us
  other arithmetic: 8.48 us -> 1.2 us
  blocking collectives: 4.94 us -> 0 us
    pallas_call x0 -> x2, Pallas kernels: none -> 113 us  [the longest x1 78.5 us: on_device(): pl.pallas_call(functools.partial(layer_kernel, (nr, nb, steps, width, par...]
    reduce_scatter x1 -> x0, waiting for transfers between devices: 61.1 us -> none  [on_device(): lax.psum_scatter(jnp.dot(hidden, down_weight, preferred_element_type=jnp....]
    psum x1 -> x0, waiting for transfers between devices: 51.2 us -> none  [on_device(): lax.psum((gate_part, up_part, squares), 'blk')]
    all_gather x1 -> x0, waiting for transfers between devices: 40 us -> none  [on_device(): gathered = lax.all_gather(local_tokens, 'rows', axis=0, tiled=True)]
    dot_general x8 -> x0, matrix products: 28.6 us -> none  [the longest x1 9.34 us: on_device(): jnp.dot(hidden, down_weight, preferred_element_type=jnp.float32)]
    all_to_all x1 -> x0, waiting for transfers between devices: 15.7 us -> none  [on_device(): lax.all_to_all(outgoing, 'rows', split_axis=0, concat_axis=0, tiled=True)]
    gather x1 -> x0, local copies, waits for them, and re-layouts: 11.8 us -> none  [on_device(): fetched = page_store[page_table]]
    unnamed x18 -> x0, local copies, waits for them, and re-layouts: 8.26 us -> none
  transfers between devices with their start and end apart: 4 -> 0, of which waited for: 4 -> 0; matrix products, arithmetic and copies ran while one was open for 3% -> 0% of each run, Pallas kernels for 0% -> 0%
where the time goes in v1:
time: 124 us; the launch traced here: 123 us
  Pallas kernels  113 us (91%)
  local copies, waits for them, and re-layouts  8.45 us (7%)
    pallas_call x1, Pallas kernels, on_device(): pl.pallas_call(functools.partial(layer_kernel, (nr, nb, steps, width, par...  78.5 us
    pallas_call x1, Pallas kernels, pack_pages(): pl.pallas_call(pack_kernel, out_shape=jax.ShapeDtypeStruct((owners * CAP,...  34.3 us
    reshape x2, local copies, waits for them, and re-layouts, on_device(): return (attended.reshape(shape), layer.reshape(shape))  3 us

profile of v1, /device:TPU:0, one launch (start us, length us, event | category | flops | bytes accessed | tf_op | source)
XLA Modules:
  0.0 123.2 jit_solution(16767041637173717312)
XLA Ops:
  0.7 0.7 copy.15
  1.4 1.3 %reshape.80.gain_ref = bf16[1,4096]{1,0:T(2,128)(2,1)} reshape(bf16[4096]{0:T(1024)(128)(2,1)} %param.18) | data formatting | bytes 16384 | tf_op jit(solution)/shard_map/reshape | solution.py:504
  2.7 1.5 %reshape.78.q_ref = bf16[8,4096]{1,0:T(8,128)(2,1)} reshape(bf16[2,4,4096]{2,1,0:T(4,128)(2,1)} %param.11) | data formatting | bytes 131072 | tf_op jit(solution)/shard_map/reshape | solution.py:504
  4.2 0.7 pad.4.new_ref
  4.9 0.1 broadcast_add_fusion
  5.0 1.1 and_reduce_fusion
  6.1 0.6 slice.9.swap_bias_ref
  6.7 0.6 slice.8.res_bias_ref
  7.3 34.3 %shard_map.122 = bf16[32,2,16,512]{3,2,1,0:T(8,128)(2,1)} custom-call(s32[16]{0:T(128)} %dest_ref.1, bf16[16,2,16,512]{3,2,1,0:T(8,128)(2,1)} %swap_ref.1), custom_call_target="tpu_custom_call" | custom-call | tf_op jit(solution)/shard_map/pallas_call | solution.py:53
  41.7 78.5 %shard_map.123 = (bf16[8,4096]{1,0:T(8,128)(2,1)}, bf16[8,4096]{1,0:T(8,128)(2,1)}) custom-call(bf16[8,4096]{1,0:T(8,128)(2,1)} %reshape.78.q_ref, bf16[2,128,512]{2,1,0:T(8,128)(2,1)} %pad.4.new_ref, f32[2,1792]{1,0:T(2,128)} %slice.8.res_bias_ref, f32[2,512]{1,0:T(2,128)} %slice.9.swap_bias_ref, bf16[1,4096]{1,0:T(2,128)(2,1)} %reshape.80.gain_ref, ...), custom_call_target="tpu_custom_call" | custom-call | flops 5637144576 | bytes 44040192 | tf_op jit(solution)/shard_map/pallas_call | solution.py:463
  120.2 1.5 %reshape.82 = bf16[2,4,4096]{2,1,0:T(4,128)(2,1)} reshape(bf16[8,4096]{1,0:T(8,128)(2,1)} %get-tuple-element.4) | data formatting | bytes 131072 | tf_op jit(solution)/shard_map/reshape | solution.py:508
  121.7 1.5 %reshape.83 = bf16[2,4,4096]{2,1,0:T(4,128)(2,1)} reshape(bf16[8,4096]{1,0:T(8,128)(2,1)} %get-tuple-element.5) | data formatting | bytes 131072 | tf_op jit(solution)/shard_map/reshape | solution.py:508
  (4 shorter events, 0.0 us)

commit v2 on v1

--- a/solution.py
+++ b/solution.py
@@ -18,59 +18,14 @@
 NEG = -1e30
 
 
-def pack_kernel(dest_ref, swap_ref, out_ref, count_ref, source_ref, sems):
-    pages = swap_ref.shape[0]
-    slots = out_ref.shape[0]
-
-    @pl.loop(0, slots)
-    def _(i):
-        source_ref[i] = 0
-
-    @pl.loop(0, slots // CAP)
-    def _(i):
-        count_ref[i] = 0
-
-    @pl.loop(0, pages)
-    def _(i):
-        owner = dest_ref[i]
-        rank = count_ref[owner]
-        count_ref[owner] = rank + 1
-        source_ref[owner * CAP + rank] = i
-
-    def copy(i):
-        return pltpu.make_async_copy(swap_ref.at[source_ref[i]], out_ref.at[i], sems.at[i])
-
-    @pl.loop(0, slots)
-    def _(i):
-        copy(i).start()
-
-    @pl.loop(0, slots)
-    def _(i):
-        copy(i).wait()
-
-
-def pack_pages(swap_dest, swap_area, owners):
-    return pl.pallas_call(
-        pack_kernel,
-        out_shape=jax.ShapeDtypeStruct((owners * CAP,) + swap_area.shape[1:], swap_area.dtype),
-        in_specs=[pl.BlockSpec(memory_space=pltpu.SMEM), pl.BlockSpec(memory_space=pl.ANY)],
-        out_specs=pl.BlockSpec(memory_space=pl.ANY),
-        scratch_shapes=[
-            pltpu.SMEM((owners,), jnp.int32),
-            pltpu.SMEM((owners * CAP,), jnp.int32),
-            pltpu.SemaphoreType.DMA((owners * CAP,)),
-        ],
-    )(swap_dest, swap_area)
-
-
 def layer_kernel(
     cfg,
-    q_ref, new_ref, res_bias_ref, swap_bias_ref, gain_ref,
-    resident_ref, outgoing_ref, wg_hbm, wu_hbm, wd_hbm,
+    source_ref, q_ref, new_ref, seen_ref, gain_ref,
+    resident_ref, swap_ref, wg_hbm, wu_hbm, wd_hbm,
     att_out, layer_out,
-    kv, arrived, wg, wu, wd, att, ag, lhs, gu32, gu16, gu_in, sq_out, sq_in, hid,
+    kv, swap_in, outgoing, arrived, wg, wu, wd, att, ag, lhs, gu32, gu16, gu_in, sq_out, sq_in, hid,
     acc, rs, rs_core, rs_y, rs_z,
-    kv_sem, w_sem, own_sem,
+    kv_sem, w_sem, swap_sem,
     sw_s, sw_r, az_s, az_r, ay_s, ay_r, ac_s, ac_r,
     gu_s, gu_r, sq_s, sq_r, hd_s, hd_r,
     rc_s, rc_r, ry_s, ry_r, rz_s, rz_r,
@@ -91,6 +46,8 @@
     def row_of(z_, y_, c_):
         return {"rows": z_ * 4 + y_ * 2 + c_}
 
+    swap_load = pltpu.make_async_copy(swap_ref, swap_in, swap_sem)
+    swap_load.start()
     kv_copy = pltpu.make_async_copy(resident_ref, kv, kv_sem)
     kv_copy.start()
 
@@ -127,15 +84,20 @@
     def swap_copy(k):
         dest = lax.rem(me + k, nr)
         return remote(
-            outgoing_ref.at[dest], arrived.at[me], sw_s.at[k], sw_r.at[k], {"rows": dest}
-        )
-
-    own_copy = pltpu.make_async_copy(outgoing_ref.at[me], arrived.at[me], own_sem)
-    own_copy.start()
+            outgoing.at[dest], arrived.at[me], sw_s.at[k], sw_r.at[k], {"rows": dest}
+        )
+
+    swap_load.wait()
 
     @pl.loop(1, nr)
     def _(k):
+        dest = lax.rem(me + k, nr)
+        for i in range(CAP):
+            outgoing[dest, i] = swap_in[source_ref[dest * CAP + i]]
         swap_copy(k).start()
+
+    for i in range(CAP):
+        arrived[me, i] = swap_in[source_ref[me * CAP + i]]
 
     for i in range(3):
         for copy in weight_copies(i):
@@ -144,10 +106,11 @@
     scale = 1.0 / math.sqrt(HD)
     token_row = lax.broadcasted_iota(jnp.int32, (TOK, 1), 0) // steps
 
-    def token_mask(ref):
-        mask = jnp.broadcast_to(ref[0:1, :], (TOK, ref.shape[1]))
+    def token_mask(first, count):
+        places = slice(first, first + count)
+        mask = jnp.broadcast_to(seen_ref[0:1, places], (TOK, count))
         for r in range(1, rows_here):
-            mask = jnp.where(token_row == r, ref[r : r + 1, :], mask)
+            mask = jnp.where(token_row == r, seen_ref[r : r + 1, places], mask)
         return mask[None] > 0.5
 
     def scores(qk, keys, mask):
@@ -168,7 +131,7 @@
         (tok_i // steps == key_i // steps) & (key_i % steps <= tok_i % steps) & (key_i < TOK)
     )[None]
 
-    q32 = q_ref[...].astype(jnp.float32)
+    q32 = jnp.concatenate([q_ref[r].astype(jnp.float32) for r in range(rows_here)], axis=0)
     heads = []
     for k in range(kh):
         heads.append(
@@ -177,8 +140,8 @@
             ).astype(jnp.bfloat16)
         )
     kv_copy.wait()
-    res_mask = token_mask(res_bias_ref)
     n_res = kv.shape[0] * PAGE
+    res_mask = token_mask(0, n_res)
     state = []
     for k in range(kh):
         lanes = slice(k * HD, (k + 1) * HD)
@@ -190,14 +153,12 @@
         o = weigh(p1, kv[:, 1, :, lanes].reshape(n_res, HD)) + weigh(p2, new_ref[1, :, lanes])
         state.append((m, l, o))
 
-    own_copy.wait()
-
     @pl.loop(1, nr)
     def _(k):
         swap_copy(k).wait_recv()
 
-    swap_mask = token_mask(swap_bias_ref)
     n_swap = nr * CAP * PAGE
+    swap_mask = token_mask(n_res, n_swap)
     for k in range(kh):
         lanes = slice(k * HD, (k + 1) * HD)
         m1, l1, o1 = state[k]
@@ -236,7 +197,8 @@
         ).astype(jnp.bfloat16)
         for k in range(1, zs):
             ag_z(n, k).start()
-    att_out[...] = att[...].astype(jnp.bfloat16)
+    for r in range(rows_here):
+        att_out[r] = att[r * steps : (r + 1) * steps, :].astype(jnp.bfloat16)
     for n in range(nt):
         for k in range(1, zs):
             ag_z(n, k).wait_recv()
@@ -383,7 +345,8 @@
             lanes = slice(side * w2 + n * tn, side * w2 + (n + 1) * tn)
             base = att[:, lanes].astype(jnp.bfloat16).astype(jnp.float32)
             att[:, lanes] = base + value[side * TOK : (side + 1) * TOK]
-    layer_out[...] = att[...].astype(jnp.bfloat16)
+    for r in range(rows_here):
+        layer_out[r] = att[r * steps : (r + 1) * steps, :].astype(jnp.bfloat16)
 
     @pl.loop(1, nr)
     def _(k):
@@ -437,7 +400,11 @@
     part = tokens // nb
     parts = 4
 
-    outgoing = pack_pages(swap_dest, swap_area, nr).reshape(nr, CAP, 2, PAGE, kvw)
+    index = jnp.arange(swap_dest.shape[0], dtype=jnp.int32)
+    same = (swap_dest[:, None] == swap_dest[None, :]) & (index[None, :] < index[:, None])
+    slot = swap_dest * CAP + jnp.sum(same.astype(jnp.int32), axis=1)
+    goes = slot[None, :] == jnp.arange(nr * CAP, dtype=jnp.int32)[:, None]
+    source = jnp.sum(jnp.where(goes, index[None, :], 0), axis=1)
 
     total_pages = res_pages + nr * CAP
     place = jnp.arange(total_pages * PAGE, dtype=jnp.int32)
@@ -447,8 +414,6 @@
         & (position[None] < lengths[:, None, None]),
         axis=1,
     ).astype(jnp.float32)
-    res_bias = seen[:, : res_pages * PAGE]
-    swap_bias = seen[:, res_pages * PAGE :]
     new_kv = jnp.pad(
         new_entries.transpose(2, 0, 1, 3).reshape(2, TOK, kvw), ((0, 0), (0, 128 - TOK), (0, 0))
     )
@@ -462,11 +427,13 @@
     pair = lambda *shape: [dma(shape), dma(shape)]
     attended, layer = pl.pallas_call(
         functools.partial(layer_kernel, (nr, nb, steps, width, parts, fc)),
-        out_shape=[jax.ShapeDtypeStruct((TOK, width), bf)] * 2,
-        in_specs=[vm] * 5 + [hbm] * 5,
+        out_shape=[jax.ShapeDtypeStruct(queries.shape, bf)] * 2,
+        in_specs=[pl.BlockSpec(memory_space=pltpu.SMEM)] + [vm] * 4 + [hbm] * 5,
         out_specs=[vm] * 2,
         scratch_shapes=[
             pltpu.VMEM(resident.shape, bf),
+            pltpu.VMEM(swap_area.shape, bf),
+            pltpu.VMEM((nr, CAP, 2, PAGE, kvw), bf),
             pltpu.VMEM((nr, CAP, 2, PAGE, kvw), bf),
             pltpu.VMEM(gate_weight.shape, bf),
             pltpu.VMEM(up_weight.shape, bf),
@@ -501,11 +468,10 @@
             transcendentals=tokens * hidden,
         ),
     )(
-        queries.reshape(TOK, width), new_kv, res_bias, swap_bias, norm_gain.reshape(1, width),
-        resident, outgoing, gate_weight, up_weight, down_weight,
+        source, queries, new_kv, seen, norm_gain.reshape(1, width),
+        resident, swap_area, gate_weight, up_weight, down_weight,
     )
-    shape = (rows_here, steps, width)
-    return attended.reshape(shape), layer.reshape(shape)
+    return attended, layer
 
 
 def solution(mesh):

time: 124 us -> 89.9 us (0.73)
  Pallas kernels: 113 us -> 78.5 us
  other arithmetic: 1.2 us -> 4.04 us
  local copies, waits for them, and re-layouts: 8.45 us -> 5.73 us
    pallas_call x1 -> x0, Pallas kernels: 34.3 us -> none  [pack_pages(): pl.pallas_call(pack_kernel, out_shape=jax.ShapeDtypeStruct((owners * CAP,...]
    reshape x3 -> x0, local copies, waits for them, and re-layouts: 4.49 us -> none  [the longest x2 3 us: on_device(): return (attended.reshape(shape), layer.reshape(shape))]
    unnamed x0 -> x2, local copies, waits for them, and re-layouts: none -> 2.98 us
    reduce_sum x0 -> x2, other arithmetic: none -> 1.57 us  [the longest x1 0.91 us: on_device(): slot = swap_dest * CAP + jnp.sum(same.astype(jnp.int32), axis=1)]
where the time goes in v2:
time: 89.9 us; the launch traced here: 88.9 us
  Pallas kernels  78.5 us (87%)
  local copies, waits for them, and re-layouts  5.73 us (6%)
  other arithmetic  4.04 us (4%)
    pallas_call x1, Pallas kernels, on_device(): pl.pallas_call(functools.partial(layer_kernel, (nr, nb, steps, width, par...  78.5 us
    unnamed x2, local copies, waits for them, and re-layouts  2.98 us

profile of v2, /device:TPU:0, one launch (start us, length us, event | category | flops | bytes accessed | tf_op | source)
XLA Modules:
  0.0 88.9 jit_solution(2536703392440522705)
XLA Ops:
  0.7 0.1 broadcast_add_fusion
  0.8 1.1 %and_reduce_fusion = pred[2,2304]{1,0:T(4,128)(4,1)S(1)} fusion(s32[64,2304]{1,0:T(8,128)S(1)} %broadcast_add_fusion, s32[2304]{0:T(1024)S(1)} %add_select_fusion, s32[2,64]{1,0:T(2,128)} %param.16, s32[2]{0:T(128)} %param.17), kind=kLoop, calls=%fused_computation | loop fusion | flops 1175040 | bytes 604168 | tf_op jit(solution)/shard_map/reduce_or | solution.py:412
  1.8 0.6 convert_element_type.9.seen_ref
  2.5 0.7 copy.15
  3.2 0.7 pad.4.new_ref
  3.9 1.3 %reshape.70.gain_ref = bf16[1,4096]{1,0:T(2,128)(2,1)} reshape(bf16[4096]{0:T(1024)(128)(2,1)} %param.18) | data formatting | bytes 16384 | tf_op jit(solution)/shard_map/reshape | solution.py:471
  5.2 0.9 %convert_reduce_fusion = s32[16]{0:T(128)S(1)} fusion(s32[16]{0:T(128)} %param.15), kind=kLoop, calls=%fused_computation.15 | loop fusion | flops 1264 | bytes 128 | tf_op jit(solution)/shard_map/reduce_sum | solution.py:405
  6.1 0.7 multiply_add_fusion
  6.8 0.7 select_reduce_fusion.source_ref
  7.4 78.5 %shard_map.122 = (bf16[2,4,4096]{2,1,0:T(4,128)(2,1)}, bf16[2,4,4096]{2,1,0:T(4,128)(2,1)}) custom-call(s32[32]{0:T(128)} %select_reduce_fusion.source_ref, bf16[2,4,4096]{2,1,0:T(4,128)(2,1)} %q_ref.1, bf16[2,128,512]{2,1,0:T(8,128)(2,1)} %pad.4.new_ref, f32[2,2304]{1,0:T(2,128)} %convert_element_type.9.seen_ref, bf16[1,4096]{1,0:T(2,128)(2,1)} %reshape.70.gain_ref, ...), custom_call_target="tpu_custom_call" | custom-call | flops 5637144576 | bytes 44040192 | tf_op jit(solution)/shard_map/pallas_call | solution.py:428
  86.0 1.5 %copy.18 = bf16[2,4,4096]{2,1,0:T(4,128)(2,1)} copy(bf16[2,4,4096]{2,1,0:T(4,128)(2,1)} %get-tuple-element.4) | data formatting | bytes 131072
  87.5 1.5 %copy.19 = bf16[2,4,4096]{2,1,0:T(4,128)(2,1)} copy(bf16[2,4,4096]{2,1,0:T(4,128)(2,1)} %get-tuple-element.5) | data formatting | bytes 131072
  (3 shorter events, 0.0 us)

commit v3 on v2

--- a/solution.py
+++ b/solution.py
@@ -81,27 +81,36 @@
             device_id=device, device_id_type=MESH,
         )
 
+    half = nr // 2
+
+    def swap_dest(k):
+        return (k // half + 1 + me // half) % 2 * half + (me + k) % half
+
     def swap_copy(k):
-        dest = lax.rem(me + k, nr)
+        dest = swap_dest(k)
         return remote(
             outgoing.at[dest], arrived.at[me], sw_s.at[k], sw_r.at[k], {"rows": dest}
         )
 
     swap_load.wait()
 
-    @pl.loop(1, nr)
-    def _(k):
-        dest = lax.rem(me + k, nr)
+    def swap_send(k):
+        dest = swap_dest(k)
         for i in range(CAP):
             outgoing[dest, i] = swap_in[source_ref[dest * CAP + i]]
         swap_copy(k).start()
 
+    pl.loop(0, half)(swap_send)
+    pl.loop(half + 1, nr)(swap_send)
+
     for i in range(CAP):
         arrived[me, i] = swap_in[source_ref[me * CAP + i]]
 
     for i in range(3):
         for copy in weight_copies(i):
             copy.start()
+
+    acc[...] = jnp.zeros_like(acc)
 
     scale = 1.0 / math.sqrt(HD)
     token_row = lax.broadcasted_iota(jnp.int32, (TOK, 1), 0) // steps
@@ -125,8 +134,13 @@
         o = jnp.dot(p2, values, preferred_element_type=jnp.float32)
         return o.reshape(GQ, TOK, HD)
 
-    tok_i = lax.broadcasted_iota(jnp.int32, (TOK, new_ref.shape[1]), 0)
-    key_i = lax.broadcasted_iota(jnp.int32, (TOK, new_ref.shape[1]), 1)
+    fresh = []
+    for i in range(2):
+        entries = [new_ref[r].astype(jnp.float32)[:, i, :] for r in range(rows_here)]
+        entries.append(jnp.zeros((128 - TOK, new_ref.shape[-1]), jnp.float32))
+        fresh.append(jnp.concatenate(entries, axis=0).astype(jnp.bfloat16))
+    tok_i = lax.broadcasted_iota(jnp.int32, (TOK, 128), 0)
+    key_i = lax.broadcasted_iota(jnp.int32, (TOK, 128), 1)
     new_mask = (
         (tok_i // steps == key_i // steps) & (key_i % steps <= tok_i % steps) & (key_i < TOK)
     )[None]
@@ -146,16 +160,15 @@
     for k in range(kh):
         lanes = slice(k * HD, (k + 1) * HD)
         s1 = scores(heads[k], kv[:, 0, :, lanes].reshape(n_res, HD), res_mask)
-        s2 = scores(heads[k], new_ref[0, :, lanes], new_mask)
+        s2 = scores(heads[k], fresh[0][:, lanes], new_mask)
         m = jnp.maximum(jnp.max(s1, axis=-1, keepdims=True), jnp.max(s2, axis=-1, keepdims=True))
         p1, p2 = jnp.exp(s1 - m), jnp.exp(s2 - m)
         l = jnp.sum(p1, axis=-1, keepdims=True) + jnp.sum(p2, axis=-1, keepdims=True)
-        o = weigh(p1, kv[:, 1, :, lanes].reshape(n_res, HD)) + weigh(p2, new_ref[1, :, lanes])
+        o = weigh(p1, kv[:, 1, :, lanes].reshape(n_res, HD)) + weigh(p2, fresh[1][:, lanes])
         state.append((m, l, o))
 
-    @pl.loop(1, nr)
-    def _(k):
-        swap_copy(k).wait_recv()
+    pl.loop(0, half)(lambda k: swap_copy(k).wait_recv())
+    pl.loop(half + 1, nr)(lambda k: swap_copy(k).wait_recv())
 
     n_swap = nr * CAP * PAGE
     swap_mask = token_mask(n_res, n_swap)
@@ -214,7 +227,7 @@
             x = wide[:, side].reshape(tokens, tn)
             squares = squares + jnp.sum(x * x, axis=1, keepdims=True)
             lanes = slice(side * w2 + n * tn, side * w2 + (n + 1) * tn)
-            lhs[:, lanes] = (x * gain_ref[:, lanes].astype(jnp.float32)).astype(jnp.bfloat16)
+            lhs[:, lanes] = (x * gain_ref[lanes].reshape(1, tn)).astype(jnp.bfloat16)
     sq_out[...] = jnp.broadcast_to(squares, sq_out.shape)
 
     def share(p):
@@ -279,11 +292,6 @@
     for copy in weight_copies(2):
         copy.wait()
 
-    @pl.loop(0, nc)
-    def _(j):
-        for k in range(1, nb):
-            hid_copy(j, k).wait_recv()
-
     def rs_c_copy(n):
         return remote(
             rs.at[n, slots((1 - c) * 2 * zs, 2 * zs)], rs_core.at[n],
@@ -303,23 +311,33 @@
             rz_s.at[n, k - 1], rz_r.at[n, k - 1], row_of(zp, y, c),
         )
 
-    def down(n, carry):
+    def down(n, j):
+        rows = pl.ds(pl.multiple_of(j * fc, fc), fc) if nc > 1 else slice(None)
         sides = []
         for side in range(2):
             cols = pl.ds(pl.multiple_of(side * w2 + n * tn, tn), tn)
-            value = jnp.zeros((tokens, tn), jnp.float32)
-            for j in range(nc):
-                value = value + jnp.dot(
-                    hid[j], wd[j * fc : (j + 1) * fc, cols], preferred_element_type=jnp.float32
-                )
+            value = jnp.dot(hid[j], wd[rows, cols], preferred_element_type=jnp.float32)
             sides.append(value.reshape(nr, TOK, tn))
-        value = jnp.concatenate(sides, axis=1).reshape(nr * 16, tn)
+        return jnp.concatenate(sides, axis=1).reshape(nr * 16, tn)
+
+    @pl.loop(0, nc - 1)
+    def _(j):
+        for k in range(1, nb):
+            hid_copy(j, k).wait_recv()
+
+        @pl.loop(0, nt)
+        def _(n):
+            acc[n] = acc[n] + down(n, j)
+
+    for k in range(1, nb):
+        hid_copy(nc - 1, k).wait_recv()
+
+    @pl.loop(0, nt)
+    def _(n):
+        value = acc[n] + down(n, nc - 1)
         acc[n] = value
         rs[n] = value.astype(jnp.bfloat16)
         rs_c_copy(n).start()
-        return carry
-
-    lax.fori_loop(0, nt, down, 0)
 
     for n in range(nt):
         rs_c_copy(n).wait_recv()
@@ -348,9 +366,8 @@
     for r in range(rows_here):
         layer_out[r] = att[r * steps : (r + 1) * steps, :].astype(jnp.bfloat16)
 
-    @pl.loop(1, nr)
-    def _(k):
-        swap_copy(k).wait_send()
+    pl.loop(0, half)(lambda k: swap_copy(k).wait_send())
+    pl.loop(half + 1, nr)(lambda k: swap_copy(k).wait_send())
 
     for k in range(1, nb):
         sq_copy(k).wait_send()
@@ -414,10 +431,6 @@
         & (position[None] < lengths[:, None, None]),
         axis=1,
     ).astype(jnp.float32)
-    new_kv = jnp.pad(
-        new_entries.transpose(2, 0, 1, 3).reshape(2, TOK, kvw), ((0, 0), (0, 128 - TOK), (0, 0))
-    )
-
     bf, f32 = jnp.bfloat16, jnp.float32
     dma = pltpu.SemaphoreType.DMA
     vm = pl.BlockSpec(memory_space=pltpu.VMEM)
@@ -468,7 +481,7 @@
             transcendentals=tokens * hidden,
         ),
     )(
-        source, queries, new_kv, seen, norm_gain.reshape(1, width),
+        source, queries, new_entries, seen, norm_gain.astype(f32),
         resident, swap_area, gate_weight, up_weight, down_weight,
     )
     return attended, layer

time: 89.9 us -> 89.7 us (level)
  local copies, waits for them, and re-layouts: 5.73 us -> 2.98 us
  Pallas kernels: 78.5 us -> 80.5 us
  other arithmetic: 4.04 us -> 5.27 us
    reshape x2 -> x0, local copies, waits for them, and re-layouts: 2.03 us -> none  [the longest x1 1.31 us: on_device(): norm_gain.reshape(1, width)]
    pallas_call x1, Pallas kernels: 78.5 us -> 80.5 us  [on_device(): pl.pallas_call(functools.partial(layer_kernel, (nr, nb, steps, width, par...]
    convert_element_type x0 -> x1, other arithmetic: none -> 1.3 us  [on_device(): norm_gain.astype(f32)]
where the time goes in v3:
time: 89.7 us; the launch traced here: 89.4 us
  Pallas kernels  80.5 us (90%)
  other arithmetic  5.27 us (6%)
  local copies, waits for them, and re-layouts  2.98 us (3%)
    pallas_call x1, Pallas kernels, on_device(): pl.pallas_call(functools.partial(layer_kernel, (nr, nb, steps, width, par...  80.5 us
    unnamed x2, local copies, waits for them, and re-layouts  2.98 us

profile of v3, /device:TPU:0, one launch (start us, length us, event | category | flops | bytes accessed | tf_op | source)
XLA Modules:
  0.0 89.4 jit_solution(14754068934672640616)
XLA Ops:
  0.7 0.1 broadcast_add_fusion
  0.8 1.1 %and_reduce_fusion = pred[2,2304]{1,0:T(4,128)(4,1)S(1)} fusion(s32[64,2304]{1,0:T(8,128)S(1)} %broadcast_add_fusion, s32[2304]{0:T(1024)S(1)} %add_select_fusion, s32[2,64]{1,0:T(2,128)} %param.16, s32[2]{0:T(128)} %param.17), kind=kLoop, calls=%fused_computation | loop fusion | flops 1175040 | bytes 604168 | tf_op jit(solution)/shard_map/reduce_or | solution.py:429
  1.8 0.6 convert_element_type.10.seen_ref
  2.5 1.3 %convert_element_type.11.gain_ref = f32[4096]{0:T(1024)} convert(bf16[4096]{0:T(1024)(128)(2,1)} %param.18) | non-fusion elementwise | flops 4096 | bytes 24576 | tf_op jit(solution)/shard_map/convert_element_type | solution.py:484
  3.8 0.9 %convert_reduce_fusion = s32[16]{0:T(128)S(1)} fusion(s32[16]{0:T(128)} %param.15), kind=kLoop, calls=%fused_computation.15 | loop fusion | flops 1264 | bytes 128 | tf_op jit(solution)/shard_map/reduce_sum | solution.py:422
  4.7 0.7 multiply_add_fusion
  5.3 0.6 select_reduce_fusion.source_ref
  5.9 80.5 %shard_map.122 = (bf16[2,4,4096]{2,1,0:T(4,128)(2,1)}, bf16[2,4,4096]{2,1,0:T(4,128)(2,1)}) custom-call(s32[32]{0:T(128)} %select_reduce_fusion.source_ref, bf16[2,4,4096]{2,1,0:T(4,128)(2,1)} %q_ref.1, bf16[2,4,2,512]{3,2,1,0:T(2,128)(2,1)} %new_ref.1, f32[2,2304]{1,0:T(2,128)} %convert_element_type.10.seen_ref, f32[4096]{0:T(1024)} %convert_element_type.11.gain_ref, ...), custom_call_target="tpu_custom_call" | custom-call | flops 5637144576 | bytes 44040192 | tf_op jit(solution)/shard_map/pallas_call | solution.py:441
  86.4 1.5 %copy.15 = bf16[2,4,4096]{2,1,0:T(4,128)(2,1)} copy(bf16[2,4,4096]{2,1,0:T(4,128)(2,1)} %get-tuple-element.4) | data formatting | bytes 131072
  87.9 1.5 %copy.16 = bf16[2,4,4096]{2,1,0:T(4,128)(2,1)} copy(bf16[2,4,4096]{2,1,0:T(4,128)(2,1)} %get-tuple-element.5) | data formatting | bytes 131072
  (3 shorter events, 0.0 us)
